TPU v7x, 128 devices: a whole 4x4x4 slice. The times are simulated.
128 devices in a mesh: ind: 16 (over x, z_hi, core), bin: 8 (over z_lo, y).
Axes of the slice: x: 4, y: 4, z: 4 (z_hi: 2, z_lo: 2; z = z_hi * 2 + z_lo), core: 2. Of those that a mesh axis runs over, the one named last changes fastest.
Arguments:
- genotype: int32 [4096, 204800], P('ind', 'bin'), may hold values from 0 to 2
- snp_mean: float32 [204800], P('bin'), may hold values from 0.9 to 1.1
- snp_scale: float32 [204800], P('bin'), may hold values from 0.75 to 0.9
- snp_label: int32 [204800], P('bin'), may hold values from 0 to 23, as said below
- probe_bits: int32 [10, 4096], P(None, 'ind'), may hold values from 0 to 1
- phenotype: bfloat16 [4096], P('ind'), may hold values from -6 to 6
Outputs:
- field: bfloat16 [24, 10, 4096], P('bin', None, 'ind')
- pair: float32 [24, 24], P('bin')
- trace: float32 [24], P('bin')
- quadratic: float32 [24], P('bin')
Inputs may be any that keep to these rules, and one draw needn't show every extreme that they name: `snp_label`: the label of SNP m lies from (m // 25600) * 3 to (m // 25600) * 3 + 2, and every bin holds at least one SNP.
All inputs are finite; a program needn't handle non-finite values.
Results may differ from a plain program's by a relative error of at most 0.0053.
Values may be sent and summed in bfloat16 or wider, within the bound.
A program may use at most 128 MiB of HBM per device.

v0:
```python
import jax
import jax.numpy as jnp
from jax import lax
from jax.sharding import PartitionSpec as P

BINS = 24
PROBES = 10


def shards(genotype, snp_mean, snp_scale, snp_label, probe_bits, phenotype):
    ind_count = lax.axis_size("ind")
    bin_count = lax.axis_size("bin")
    own_bins = BINS // bin_count
    first_bin = lax.axis_index("bin") * own_bins
    rows = genotype.shape[0]
    snps = genotype.shape[1]
    total_rows = rows * ind_count
    stand = ((genotype.astype(jnp.float32) - snp_mean[None, :]) / snp_scale[None, :]).astype(
        jnp.bfloat16
    )
    probes = (2 * probe_bits - 1).astype(jnp.bfloat16)
    left = jnp.concatenate([probes, phenotype[None, :]], axis=0)
    partial_value = jnp.dot(left, stand, preferred_element_type=jnp.float32)
    local_label = snp_label - first_bin
    bin_ids = jnp.arange(own_bins, dtype=jnp.int32)[:, None]
    member = local_label[None, :] == bin_ids
    count = jnp.sum(member.astype(jnp.float32), axis=1)
    squares = jnp.sum(jnp.square(stand.astype(jnp.float32)), axis=0)
    trace_part = jnp.sum(jnp.where(member, squares[None, :], 0.0), axis=1)
    totals = lax.psum(partial_value, "ind")
    trait = totals[PROBES]
    quad_whole = jnp.sum(jnp.where(member, (trait * trait)[None, :], 0.0), axis=1)
    weights = totals[:PROBES].astype(jnp.bfloat16)
    expanded = jnp.where(member[:, None, :], weights[None, :, :], jnp.zeros((), jnp.bfloat16))
    expanded = expanded.reshape(own_bins * PROBES, snps)
    hidden = lax.dot_general(
        expanded, stand, (((1,), (1,)), ((), ())), preferred_element_type=jnp.float32
    )
    field = (hidden.reshape(own_bins, PROBES, rows) / count[:, None, None]).astype(jnp.bfloat16)
    own_flat = field.reshape(own_bins, PROBES * rows)
    piece = lax.all_gather(field, "bin", axis=0, tiled=True)
    other = piece.reshape(piece.shape[0], PROBES * rows)
    pair_part = lax.dot_general(
        own_flat, other, (((1,), (1,)), ((), ())), preferred_element_type=jnp.float32
    )
    pair_total, trace_total = lax.psum((pair_part, trace_part), "ind")
    pair = pair_total / (PROBES * total_rows)
    trace = trace_total / (count * total_rows)
    quadratic = quad_whole / (count * total_rows)
    return (field, pair, trace, quadratic)


def solution(mesh):
    placed = (P("ind", "bin"), P("bin"), P("bin"), P("bin"), P(None, "ind"), P("ind"))
    return jax.shard_map(
        shards,
        mesh=mesh,
        in_specs=placed,
        out_specs=(P("bin", None, "ind"), P("bin", None), P("bin"), P("bin")),
        check_vma=False,
    )
```

profile of v0, /device:TPU:1, one launch (start us, length us, event | category | flops | bytes accessed | tf_op | source)
XLA Modules:
  0.0 255.9 jit_solution(519928032652095972)
XLA Ops:
  7.2 0.0 all-reduce.3.cloned.1.call-start
  7.2 0.7 add_convert_fusion
  7.9 0.7 broadcast_in_dim.53
  8.6 12.0 %multiply_reduce_fusion = (f32[25600]{0:T(1024)S(1)}, bf16[256,25600]{1,0:T(8,128)(2,1)S(1)}) fusion(f32[25600]{0:T(1024)} %param.8, f32[25600]{0:T(1024)} %param.7, s32[256,25600]{1,0:T(8,128)} %param.6), kind=kLoop, calls=%fused_computation | loop fusion | flops 45849600 | bytes 39628800 | tf_op jit(solution)/shard_map/reduce_sum | solution.py:28
  20.6 0.0 copy-start
  20.6 0.0 copy-start.1
  20.6 4.6 %copy-done = bf16[256,25600]{1,0:T(8,128)(2,1)} copy-done((bf16[256,25600]{1,0:T(8,128)(2,1)}, bf16[256,25600]{1,0:T(8,128)(2,1)S(1)}, u32[]{:S(2)}) %copy-start) | copy-done | bytes 13107224
  25.3 3.0 %fusion.17 = f32[11,25600]{1,0:T(8,128)} fusion(bf16[256,25600]{1,0:T(8,128)(2,1)S(1)} %get-tuple-element.19, bf16[1,256]{1,0:T(2,128)(2,1)S(1)} %broadcast_in_dim.53, bf16[10,256]{1,0:T(8,128)(2,1)S(1)} %add_convert_fusion), kind=kOutput, calls=%fused_computation.20 | convolution fusion | flops 144190464 | bytes 14239232 | tf_op jit(solution)/shard_map/dot_general | solution.py:23
  28.3 0.0 all-reduce.3.cloned.1.call-update
  28.3 0.0 copy-done.1
  28.3 146.1 %all-reduce.3.cloned.1.call-done = f32[11,25600]{1,0:T(8,128)} async-done(((f32[11,25600]{1,0:T(8,128)}), f32[11,25600]{1,0:T(8,128)}) %all-reduce.3.cloned.1.call-update) | async-done | bytes 1126416 | tf_op jit(solution)/shard_map/psum | solution.py:30
  174.4 1.2 slice_multiply_fusion
  175.7 0.6 select_reduce_fusion
  176.2 1.5 slice.13
  177.7 8.8 %fusion.11 = bf16[3,10,256]{2,1,0:T(8,128)(2,1)S(1)} fusion(bf16[256,25600]{1,0:T(8,128)(2,1)} %copy-done, pred[3,25600]{1,0:T(4,128)(4,1)S(1)} %get-tuple-element.17, bf16[10,25600]{1,0:T(8,128)(2,1)S(1)} %slice.13, f32[3]{0:T(128)S(1)} %get-tuple-element.14), kind=kOutput, calls=%fused_computation.10 | convolution fusion | flops 393999360 | bytes 13711372 | tf_op jit(solution)/shard_map/dot_general | solution.py:36
  186.5 0.0 copy-start.2
  186.5 21.9 %all_gather.3 = bf16[24,10,256]{2,1,0:T(8,128)(2,1)S(1)} all-gather(bf16[3,10,256]{2,1,0:T(8,128)(2,1)S(1)} %fusion.11), channel_id=1, replica_groups=mesh['ind'=16,'bin'=8] {'bin'}, dimensions={0}, use_global_device_ids=true | all-gather | bytes 138240 | tf_op jit(solution)/shard_map/all_gather | solution.py:41
  208.5 0.2 convolution_bitcast_fusion
  208.6 39.3 %all-reduce = (f32[3,24]{1,0:T(4,128)S(1)}, f32[3]{0:T(128)S(1)}) all-reduce(f32[3,24]{1,0:T(4,128)S(1)} %convolution_bitcast_fusion, f32[3]{0:T(128)S(1)} %get-tuple-element.13), channel_id=1, replica_groups=mesh['ind'=16,'bin'=8] {'ind'}, use_global_device_ids=true, to_apply=%region_2.3 | all-reduce | flops 75 | bytes 600 | tf_op jit(solution)/shard_map/psum | solution.py:46
  247.9 0.6 broadcast_multiply_fusion
  248.5 0.5 multiply_divide_fusion
  249.1 0.0 copy-done.2
  (2 shorter events, 0.0 us)
Async XLA Ops:
  7.2 167.3 %all-reduce.3.cloned.1.call-start = ((), (), s32[]{:S(2)}) async-start(), calls=%async_computation | async-start | bytes 3276800 | tf_op jit(solution)/shard_map/psum | solution.py:30
  20.6 4.7 %copy-start = (bf16[256,25600]{1,0:T(8,128)(2,1)}, bf16[256,25600]{1,0:T(8,128)(2,1)S(1)}, u32[]{:S(2)}) copy-start(bf16[256,25600]{1,0:T(8,128)(2,1)S(1)} %get-tuple-element.19) | copy-start | bytes 39321604
  20.6 7.7 %copy-start.1 = (s32[25600]{0:T(1024)S(1)}, s32[25600]{0:T(1024)}, u32[]{:S(2)}) copy-start(s32[25600]{0:T(1024)} %param.9) | copy-start | bytes 307204
  186.5 62.5 %copy-start.2 = (bf16[3,10,256]{2,0,1:T(4,128)(2,1)}, bf16[3,10,256]{2,0,1:T(4,128)(2,1)S(1)}, u32[]{:S(2)}) copy-start(bf16[3,10,256]{2,0,1:T(4,128)(2,1)S(1)} %copy.15) | copy-start | bytes 46084
Sparse Core Ops, SparseCore 0:
  28.4 145.9 all-reduce.2
where the time goes:
time: 256 us
  waiting for transfers between devices  146 us (57%)
  blocking collectives  61.3 us (24%)
  other arithmetic  15.6 us (6%)
  between operations  14.1 us (6%)
  matrix products  11.9 us (5%)
  local copies, waits for them, and re-layouts  6.84 us (3%)
    psum x1, waiting for transfers between devices, shards(): totals = lax.psum(partial_value, 'ind')  146 us
    psum x1, blocking collectives, shards(): pair_total, trace_total = lax.psum((pair_part, trace_part), 'ind')  39.3 us
    all_gather x1, blocking collectives, shards(): piece = lax.all_gather(field, 'bin', axis=0, tiled=True)  21.9 us
    reduce_sum x1, other arithmetic, shards(): squares = jnp.sum(jnp.square(stand.astype(jnp.float32)), axis=0)  12 us
    dot_general x1, matrix products, shards(): lax.dot_general(expanded, stand, (((1,), (1,)), ((), ())), preferred_elem...  8.75 us
  transfers between devices with their start and end apart: 1, of which 1 were waited for; matrix products, arithmetic and copies ran while one was open for 0% of the time, Pallas kernels for 0%

commit v1 on v0

v1 whole, which is shorter than its diff:
```python
import functools

import jax
import jax.numpy as jnp
from jax import lax
from jax.experimental import pallas as pl
from jax.experimental.pallas import tpu as pltpu
from jax.sharding import PartitionSpec as P

BINS = 24
PROBES = 10
OWN = 3
ROWS = 256
SNPS = 25600
INDIVIDUALS = 4096
UNIT = 2048
PADDED = 26624
UNITS = 13
SUB = 256
GROUPS = ((0, 5), (5, 4), (9, 2), (11, 2))
F32 = jnp.float32
BF16 = jnp.bfloat16
MESH = pl.DeviceIdType.MESH


def split_dot(a, b):
    high = a.astype(BF16)
    low = (a - high.astype(F32)).astype(BF16)
    both = jnp.concatenate([high, low], axis=0)
    return jnp.dot(both, b, preferred_element_type=F32)


def kernel(
    geno, mean, scale, label, probes, pheno,
    field_out, pair_out, trace_out, quad_out,
    gbuf, stand, part, other, sums, arrived, weights,
    mean_v, inv_v, label_v, left_f, left_b, squares, quads, hidden, dense, fields, messages, pick,
    g_sem, s_sem, core_send, core_recv, rs_send, rs_recv, ag_send, ag_recv, half_send, half_recv,
    f_send, f_recv, m_send, m_recv,
):
    ind = lax.axis_index("ind")
    bin_ = lax.axis_index("bin")
    core = lax.rem(ind, 2)
    chip = ind // 2
    cx, cz = chip // 2, lax.rem(chip, 2)
    first = bin_ * OWN

    small = [
        pltpu.make_async_copy(mean, mean_v, s_sem.at[0]),
        pltpu.make_async_copy(scale, inv_v, s_sem.at[1]),
        pltpu.make_async_copy(label, label_v.at[:, 0:SNPS], s_sem.at[2]),
    ]
    for copy in small:
        copy.start()

    def geno_copy(u):
        at = pl.ds(pl.multiple_of(u * UNIT, UNIT), UNIT)
        return pltpu.make_async_copy(geno.at[:, at], gbuf.at[:, at], g_sem.at[u])

    last_at = pl.ds((UNITS - 1) * UNIT, SNPS - (UNITS - 1) * UNIT)
    last_copy = pltpu.make_async_copy(geno.at[:, last_at], gbuf.at[:, last_at], g_sem.at[UNITS - 1])
    for u in range(UNITS - 1):
        geno_copy(u).start()
    last_copy.start()

    barrier = pltpu.get_barrier_semaphore()
    for d in range(1, 16):
        pl.semaphore_signal(
            barrier, inc=1, device_id=(lax.rem(ind + d, 16), bin_), device_id_type=MESH
        )
    for d in range(1, 8):
        pl.semaphore_signal(
            barrier, inc=1, device_id=(ind, lax.rem(bin_ + d, 8)), device_id_type=MESH
        )

    left_f[...] = jnp.zeros_like(left_f)
    left_f[0:PROBES, :] = (2 * probes[...] - 1).astype(F32)
    left_f[PROBES : PROBES + 1, :] = pheno[...].astype(F32)
    left_b[...] = left_f[...].astype(BF16)
    part[:, SNPS:PADDED] = jnp.zeros((16, PADDED - SNPS), F32)
    label_v[:, SNPS:PADDED] = jnp.full((1, PADDED - SNPS), -1, jnp.int32)
    squares[...] = jnp.zeros_like(squares)
    quads[...] = jnp.zeros_like(quads)
    hidden[...] = jnp.zeros_like(hidden)
    for copy in small:
        copy.wait()
    inv_v[...] = 1.0 / inv_v[...]

    def moments(start, count):
        def sub(s, carry):
            off = pl.multiple_of(start + s * SUB, SUB)
            at = pl.ds(off, SUB)
            x = ((gbuf[:, at].astype(F32) - mean_v[:, at]) * inv_v[:, at]).astype(BF16)
            stand[:, at] = x
            part[:, at] = jnp.dot(left_b[...], x, preferred_element_type=F32)
            wide = x.astype(F32)
            sq = jnp.sum((wide * wide).reshape(ROWS // 8, 8, SUB), axis=0)
            lab = label_v[:, at]
            return tuple(
                carry[k] + jnp.where(lab == first + k, sq, 0.0) for k in range(OWN)
            )

        carry = lax.fori_loop(0, count, sub, tuple(squares[k] for k in range(OWN)))
        for k in range(OWN):
            squares[k] = carry[k]

    def unit_moments(u, _):
        geno_copy(u).wait()
        moments(u * UNIT, UNIT // SUB)
        return 0

    def units(lo, hi):
        lax.fori_loop(lo, min(hi, UNITS - 1), unit_moments, 0)
        if hi == UNITS:
            last_copy.wait()
            moments((UNITS - 1) * UNIT, (SNPS - (UNITS - 1) * UNIT) // SUB)

    def half_at(g, which):
        begin, n = GROUPS[g]
        half = n * UNIT // 2
        return pl.ds(pl.multiple_of(begin * UNIT + which * half, 1024), half)

    def piece_at(g, who):
        begin, n = GROUPS[g]
        half, piece = n * UNIT // 2, n * UNIT // 16
        return pl.ds(pl.multiple_of(begin * UNIT + core * half + who * piece, 128), piece)

    def partner():
        return (chip * 2 + 1 - core, bin_)

    def core_copy(g):
        at = half_at(g, 1 - core)
        return pltpu.make_async_remote_copy(
            src_ref=part.at[:, at], dst_ref=other.at[:, at],
            send_sem=core_send.at[g], recv_sem=core_recv.at[g],
            device_id=partner(), device_id_type=MESH,
        )

    hops = ((2, 1), (1, 1), (3, 1), (2, 0), (0, 1), (1, 0), (3, 0))

    def chip_at(hop):
        return lax.rem(cx + hop[0], 4) * 2 + lax.rem(cz + hop[1], 2)

    def slots(g):
        begin, n = GROUPS[g]
        return pl.ds(begin * 128, n * 128)

    def scatter(g):
        pltpu.make_async_copy(part.at[:, half_at(g, 1 - core)], other.at[:, half_at(g, core)], core_recv.at[g]).wait()
        at = half_at(g, core)
        sums[:, at] = (part[:, at] + other[:, at]).astype(BF16)
        for slot, hop in enumerate(hops):
            who = chip_at(hop)
            pltpu.make_async_remote_copy(
                src_ref=sums.at[:, piece_at(g, who)], dst_ref=arrived.at[slot, :, slots(g)],
                send_sem=rs_send.at[g], recv_sem=rs_recv.at[g],
                device_id=(who * 2 + core, bin_), device_id_type=MESH,
            ).start()

    def all_slots(g):
        return arrived.at[:, :, slots(g)]

    def gather(g):
        pltpu.make_async_copy(all_slots(g), all_slots(g), rs_recv.at[g]).wait()
        mine = piece_at(g, chip)
        total = part[:, mine] + other[:, mine]
        for slot in range(7):
            total = total + arrived[slot, :, slots(g)].astype(F32)
        weights[:, mine] = total.astype(BF16)
        for hop in hops:
            who = chip_at(hop)
            pltpu.make_async_remote_copy(
                src_ref=weights.at[:, mine], dst_ref=weights.at[:, mine],
                send_sem=ag_send.at[g], recv_sem=ag_recv.at[g],
                device_id=(who * 2 + core, bin_), device_id_type=MESH,
            ).start()
        trait = total[8:16, :]
        row = lax.broadcasted_iota(jnp.int32, trait.shape, 0)
        trait = jnp.where(row == PROBES - 8, trait * trait, 0.0)
        lab = label_v[:, mine]
        for k in range(OWN):
            own = jnp.where(lab == first + k, trait, 0.0)
            add = quads[k]
            for t in range(own.shape[1] // 128):
                add = add + own[:, t * 128 : (t + 1) * 128]
            quads[k] = add

    def seven(g):
        begin, n = GROUPS[g]
        half, piece = n * UNIT // 2, n * UNIT // 16
        return weights.at[:, pl.ds(pl.multiple_of(begin * UNIT + core * half, 1024), 7 * piece)]

    def half_copy(g):
        at = half_at(g, core)
        return pltpu.make_async_remote_copy(
            src_ref=weights.at[:, at], dst_ref=weights.at[:, at],
            send_sem=half_send.at[g], recv_sem=half_recv.at[g],
            device_id=partner(), device_id_type=MESH,
        )

    def share(g):
        pltpu.make_async_copy(seven(g), seven(g), ag_recv.at[g]).wait()
        half_copy(g).start()

    def apply(g):
        there = weights.at[:, half_at(g, 1 - core)]
        pltpu.make_async_copy(there, there, half_recv.at[g]).wait()
        begin, n = GROUPS[g]
        start = begin * UNIT
        stop = min(start + n * UNIT, SNPS)

        def sub(s, acc):
            at = pl.ds(pl.multiple_of(start + s * SUB, SUB), SUB)
            w = weights[:, at].astype(F32)
            lab = label_v[:, at]
            e = jnp.concatenate(
                [jnp.where(lab == first + k, w, 0.0).astype(BF16) for k in range(OWN)], axis=0
            )
            return acc + lax.dot_general(
                e, stand[:, at], (((1,), (1,)), ((), ())), preferred_element_type=F32
            )

        hidden[...] = lax.fori_loop(0, (stop - start) // SUB, sub, hidden[...])

    units(0, 5)
    pl.semaphore_wait(barrier, 22)
    core_copy(0).start()
    units(5, 7)
    scatter(0)
    units(7, 9)
    core_copy(1).start()
    units(9, 11)
    scatter(1)
    core_copy(2).start()
    units(11, 12)
    scatter(2)
    units(12, 13)
    core_copy(3).start()

    def pick_table():
        c = lax.broadcasted_iota(jnp.int32, (256, 128), 0)
        lane = lax.broadcasted_iota(jnp.int32, (256, 128), 1)
        inner = c & 31
        which = (c >> 5) * OWN + (inner >= 10).astype(jnp.int32) + (inner >= 20).astype(jnp.int32)
        which = jnp.where(inner < 30, which, -1000)
        for k in range(OWN):
            pick[k * 256 : (k + 1) * 256, :] = (lane == which + BINS * k).astype(F32).astype(BF16)

    pick_table()
    lab_row = label_v[:, 0:SNPS]
    counts = [
        jnp.sum((lab_row == first + k).astype(F32), axis=1, keepdims=True) for k in range(OWN)
    ]
    scatter(3)
    gather(0)
    gather(1)
    gather(2)
    gather(3)
    share(0)
    share(1)
    apply(0)
    share(2)
    apply(1)
    share(3)
    apply(2)
    apply(3)

    dense[...] = jnp.zeros_like(dense)
    for k in range(OWN):
        f = hidden[16 * k : 16 * k + PROBES, :] / counts[k]
        field_out[k] = f.astype(BF16)
        dense[PROBES * k : PROBES * (k + 1), :] = f
    fields[pl.ds(bin_, 1)] = dense[...].astype(BF16)[None]
    for d in (4, 3, 5, 2, 6, 1, 7):
        pltpu.make_async_remote_copy(
            src_ref=fields.at[bin_], dst_ref=fields.at[bin_],
            send_sem=f_send.at[0], recv_sem=f_recv.at[0],
            device_id=(ind, lax.rem(bin_ + d, 8)), device_id_type=MESH,
        ).start()

    lane = lax.broadcasted_iota(jnp.int32, (128, 128), 1)
    extra = jnp.zeros((16, 128), F32)
    for k in range(OWN):
        tr = squares[k][:, 0:128] + squares[k][:, 128:256]
        extra = extra + split_dot(tr, (lane == 72 + k).astype(F32).astype(BF16))
        extra = extra + split_dot(quads[k], (lane == 75 + k).astype(F32).astype(BF16))
    extra = extra[0:8] + extra[8:16]

    seven_fields = fields.at[0:7]
    pltpu.make_async_copy(seven_fields, seven_fields, f_recv.at[0]).wait()
    own = fields[pl.ds(bin_, 1)].reshape(32, ROWS)
    every = fields[...].reshape(256, ROWS)
    gram = lax.dot_general(own, every, (((1,), (1,)), ((), ())), preferred_element_type=F32)
    r = lax.broadcasted_iota(jnp.int32, (32, 256), 0)
    c = lax.broadcasted_iota(jnp.int32, (32, 256), 1) & 31
    rk = (r >= 10).astype(jnp.int32) + (r >= 20).astype(jnp.int32)
    ck = (c >= 10).astype(jnp.int32) + (c >= 20).astype(jnp.int32)
    gram = jnp.where(r - 10 * rk == c - 10 * ck, gram, 0.0)
    by_bin = jnp.concatenate([jnp.where(rk == k, gram, 0.0) for k in range(OWN)], axis=1)
    pairs = split_dot(by_bin, pick[...])
    message = jnp.sum(pairs.reshape(8, 8, 128), axis=0) + extra
    messages[pl.ds(ind, 1)] = message[None]
    for d in (8, 7, 9, 6, 10, 5, 11, 4, 12, 3, 13, 2, 14, 1, 15):
        pltpu.make_async_remote_copy(
            src_ref=messages.at[ind], dst_ref=messages.at[ind],
            send_sem=m_send.at[0], recv_sem=m_recv.at[0],
            device_id=(lax.rem(ind + d, 16), bin_), device_id_type=MESH,
        ).start()

    for g in range(len(GROUPS)):
        core_copy(g).wait_send()
        pltpu.make_async_copy(all_slots(g), all_slots(g), rs_send.at[g]).wait()
        pltpu.make_async_copy(seven(g), seven(g), ag_send.at[g]).wait()
        half_copy(g).wait_send()
    pltpu.make_async_copy(seven_fields, seven_fields, f_send.at[0]).wait()

    fifteen = messages.at[0:15]
    pltpu.make_async_copy(fifteen, fifteen, m_recv.at[0]).wait()
    total = messages[0]
    for i in range(1, 16):
        total = total + messages[i]
    total = jnp.sum(total, axis=0, keepdims=True)
    for k in range(OWN):
        pair_out[k : k + 1, :] = total[:, BINS * k : BINS * (k + 1)] / (PROBES * INDIVIDUALS)
        trace_out[:, k : k + 1] = total[:, 72 + k : 73 + k] / (counts[k] * INDIVIDUALS)
        quad_out[:, k : k + 1] = total[:, 75 + k : 76 + k] / (counts[k] * INDIVIDUALS)
    pltpu.make_async_copy(fifteen, fifteen, m_send.at[0]).wait()


def shards(genotype, snp_mean, snp_scale, snp_label, probe_bits, phenotype):
    anywhere = pl.BlockSpec(memory_space=pl.ANY)
    vmem = pl.BlockSpec(memory_space=pltpu.VMEM)
    dma = pltpu.SemaphoreType.DMA
    n = len(GROUPS)
    field, pair, trace, quad = pl.pallas_call(
        kernel,
        name="moments_and_fields",
        out_shape=(
            jax.ShapeDtypeStruct((OWN, PROBES, ROWS), BF16),
            jax.ShapeDtypeStruct((OWN, BINS), F32),
            jax.ShapeDtypeStruct((1, OWN), F32),
            jax.ShapeDtypeStruct((1, OWN), F32),
        ),
        in_specs=[anywhere] * 4 + [vmem] * 2,
        out_specs=(vmem,) * 4,
        scratch_shapes=[
            pltpu.VMEM((ROWS, SNPS), jnp.int32),
            pltpu.VMEM((ROWS, SNPS), BF16),
            pltpu.VMEM((16, PADDED), F32),
            pltpu.VMEM((16, PADDED), F32),
            pltpu.VMEM((16, PADDED), BF16),
            pltpu.VMEM((7, 16, PADDED // 16), BF16),
            pltpu.VMEM((16, PADDED), BF16),
            pltpu.VMEM((1, SNPS), F32),
            pltpu.VMEM((1, SNPS), F32),
            pltpu.VMEM((1, PADDED), jnp.int32),
            pltpu.VMEM((16, ROWS), F32),
            pltpu.VMEM((16, ROWS), BF16),
            pltpu.VMEM((OWN, 8, SUB), F32),
            pltpu.VMEM((OWN, 8, 128), F32),
            pltpu.VMEM((16 * OWN, ROWS), F32),
            pltpu.VMEM((32, ROWS), F32),
            pltpu.VMEM((8, 32, ROWS), BF16),
            pltpu.VMEM((16, 8, 128), F32),
            pltpu.VMEM((768, 128), BF16),
            dma((UNITS,)), dma((3,)),
            dma((n,)), dma((n,)), dma((n,)), dma((n,)), dma((n,)), dma((n,)), dma((n,)), dma((n,)),
            dma((1,)), dma((1,)), dma((1,)), dma((1,)),
        ],
        compiler_params=pltpu.CompilerParams(
            collective_id=0, has_side_effects=True, vmem_limit_bytes=58 * 2**20
        ),
        cost_estimate=pl.CostEstimate(
            flops=2 * 64 * ROWS * SNPS, bytes_accessed=4 * ROWS * SNPS, transcendentals=0
        ),
    )(
        genotype,
        snp_mean.reshape(1, -1),
        snp_scale.reshape(1, -1),
        snp_label.reshape(1, -1),
        probe_bits,
        phenotype.reshape(1, -1),
    )
    return field, pair, trace.reshape(-1), quad.reshape(-1)


def solution(mesh):
    placed = (P("ind", "bin"), P("bin"), P("bin"), P("bin"), P(None, "ind"), P("ind"))
    return jax.shard_map(
        shards,
        mesh=mesh,
        in_specs=placed,
        out_specs=(P("bin", None, "ind"), P("bin", None), P("bin"), P("bin")),
        check_vma=False,
    )
```

time: 256 us -> 77.5 us (0.30)
  waiting for transfers between devices: 146 us -> 0 us
  Pallas kernels: 0 us -> 70.5 us
  blocking collectives: 61.3 us -> 0 us
  other arithmetic: 15.6 us -> 0 us
  between operations: 14.1 us -> 0.64 us
  matrix products: 11.9 us -> 0 us
    psum x1 -> x0, waiting for transfers between devices: 146 us -> none  [shards(): totals = lax.psum(partial_value, 'ind')]
    pallas_call x0 -> x1, Pallas kernels: none -> 70.5 us  [shards(): pl.pallas_call(kernel, name='moments_and_fields', out_shape=(jax.ShapeDty...]
    psum x1 -> x0, blocking collectives: 39.3 us -> none  [shards(): pair_total, trace_total = lax.psum((pair_part, trace_part), 'ind')]
    all_gather x1 -> x0, blocking collectives: 21.9 us -> none  [shards(): piece = lax.all_gather(field, 'bin', axis=0, tiled=True)]
    reduce_sum x2 -> x0, other arithmetic: 12.5 us -> none  [the longest x1 12 us: shards(): squares = jnp.sum(jnp.square(stand.astype(jnp.float32)), axis=0)]
    dot_general x3 -> x0, matrix products: 11.9 us -> none  [the longest x1 8.75 us: shards(): lax.dot_general(expanded, stand, (((1,), (1,)), ((), ())), preferred_elem...]
  transfers between devices with their start and end apart: 1 -> 0, of which waited for: 1 -> 0; matrix products, arithmetic and copies ran while one was open for 0% -> 0% of each run, Pallas kernels for 0% -> 0%
where the time goes in v1:
time: 77.5 us; the launch traced here: 77.2 us
  Pallas kernels  70.5 us (91%)
  local copies, waits for them, and re-layouts  6.08 us (8%)
    pallas_call x1, Pallas kernels, shards(): pl.pallas_call(kernel, name='moments_and_fields', out_shape=(jax.ShapeDty...  70.5 us
    unnamed x4, local copies, waits for them, and re-layouts  4.86 us

profile of v1, /device:TPU:1, one launch (start us, length us, event | category | flops | bytes accessed | tf_op | source)
XLA Modules:
  0.0 77.2 jit_solution(16995658713341699008)
XLA Ops:
  0.6 1.2 %reshape.29.pheno = bf16[1,256]{1,0:T(2,128)(2,1)} reshape(bf16[256]{0:T(256)(128)(2,1)} %param.11) | data formatting | bytes 1024 | tf_op jit(solution)/shard_map/reshape | solution.py:382
  1.9 70.5 %moments_and_fields.1 = (bf16[3,10,256]{2,1,0:T(8,128)(2,1)}, f32[3,24]{1,0:T(4,128)}, f32[1,3]{1,0:T(1,128)}, f32[1,3]{1,0:T(1,128)}) custom-call(s32[256,25600]{1,0:T(8,128)} %geno.1, f32[1,25600]{1,0:T(1,128)} %bitcast.5, f32[1,25600]{1,0:T(1,128)} %bitcast.6, s32[1,25600]{1,0:T(1,128)} %bitcast.7, s32[10,256]{1,0:T(8,128)} %probes.1, ...), custom_call_target="tpu_custom_call" | custom-call | flops 838860800 | bytes 26214400 | tf_op jit(solution)/shard_map/moments_and_fields/pallas_call | solution.py:335
  72.3 1.4 %copy.10 = bf16[3,10,256]{2,0,1:T(4,128)(2,1)} copy(bf16[3,10,256]{2,1,0:T(8,128)(2,1)} %get-tuple-element.12) | data formatting | bytes 30720
  73.7 1.2 %copy.14 = f32[3,24]{1,0:T(4,128)} copy(f32[3,24]{1,0:T(4,128)} %get-tuple-element.21) | data formatting | bytes 576
  74.9 1.1 %copy.15 = f32[3]{0:T(128)} copy(f32[3]{0:T(128)} %bitcast.9) | data formatting | bytes 24
  76.1 1.1 %copy.16 = f32[3]{0:T(128)} copy(f32[3]{0:T(128)} %bitcast.8) | data formatting | bytes 24

commit v2 on v1

--- a/solution.py
+++ b/solution.py
@@ -16,8 +16,9 @@
 UNIT = 2048
 PADDED = 26624
 UNITS = 13
-SUB = 256
-GROUPS = ((0, 5), (5, 4), (9, 2), (11, 2))
+AHEAD = 3
+GROUPS = ((0, 3), (3, 3), (6, 3), (9, 2), (11, 2))
+DIRECT = (2, 3, 4)
 F32 = jnp.float32
 BF16 = jnp.bfloat16
 MESH = pl.DeviceIdType.MESH
@@ -34,7 +35,7 @@
     geno, mean, scale, label, probes, pheno,
     field_out, pair_out, trace_out, quad_out,
     gbuf, stand, part, other, sums, arrived, weights,
-    mean_v, inv_v, label_v, left_f, left_b, squares, quads, hidden, dense, fields, messages, pick,
+    mean_v, inv_v, label_v, probes_v, pheno_v, left_f, left_b, squares, quads, hidden, dense, fields, messages, pick,
     g_sem, s_sem, core_send, core_recv, rs_send, rs_recv, ag_send, ag_recv, half_send, half_recv,
     f_send, f_recv, m_send, m_recv,
 ):
@@ -49,6 +50,8 @@
         pltpu.make_async_copy(mean, mean_v, s_sem.at[0]),
         pltpu.make_async_copy(scale, inv_v, s_sem.at[1]),
         pltpu.make_async_copy(label, label_v.at[:, 0:SNPS], s_sem.at[2]),
+        pltpu.make_async_copy(probes, probes_v, s_sem.at[3]),
+        pltpu.make_async_copy(pheno, pheno_v, s_sem.at[4]),
     ]
     for copy in small:
         copy.start()
@@ -59,9 +62,8 @@
 
     last_at = pl.ds((UNITS - 1) * UNIT, SNPS - (UNITS - 1) * UNIT)
     last_copy = pltpu.make_async_copy(geno.at[:, last_at], gbuf.at[:, last_at], g_sem.at[UNITS - 1])
-    for u in range(UNITS - 1):
+    for u in range(AHEAD):
         geno_copy(u).start()
-    last_copy.start()
 
     barrier = pltpu.get_barrier_semaphore()
     for d in range(1, 16):
@@ -73,10 +75,6 @@
             barrier, inc=1, device_id=(ind, lax.rem(bin_ + d, 8)), device_id_type=MESH
         )
 
-    left_f[...] = jnp.zeros_like(left_f)
-    left_f[0:PROBES, :] = (2 * probes[...] - 1).astype(F32)
-    left_f[PROBES : PROBES + 1, :] = pheno[...].astype(F32)
-    left_b[...] = left_f[...].astype(BF16)
     part[:, SNPS:PADDED] = jnp.zeros((16, PADDED - SNPS), F32)
     label_v[:, SNPS:PADDED] = jnp.full((1, PADDED - SNPS), -1, jnp.int32)
     squares[...] = jnp.zeros_like(squares)
@@ -84,36 +82,53 @@
     hidden[...] = jnp.zeros_like(hidden)
     for copy in small:
         copy.wait()
+    left_f[...] = jnp.zeros_like(left_f)
+    left_f[0:PROBES, :] = (2 * probes_v[...] - 1).astype(F32)
+    left_f[PROBES : PROBES + 1, :] = pheno_v[...].astype(F32).reshape(1, ROWS)
+    left_b[...] = left_f[...].astype(BF16)
     inv_v[...] = 1.0 / inv_v[...]
 
-    def moments(start, count):
-        def sub(s, carry):
-            off = pl.multiple_of(start + s * SUB, SUB)
-            at = pl.ds(off, SUB)
-            x = ((gbuf[:, at].astype(F32) - mean_v[:, at]) * inv_v[:, at]).astype(BF16)
-            stand[:, at] = x
-            part[:, at] = jnp.dot(left_b[...], x, preferred_element_type=F32)
-            wide = x.astype(F32)
-            sq = jnp.sum((wide * wide).reshape(ROWS // 8, 8, SUB), axis=0)
-            lab = label_v[:, at]
-            return tuple(
-                carry[k] + jnp.where(lab == first + k, sq, 0.0) for k in range(OWN)
-            )
-
-        carry = lax.fori_loop(0, count, sub, tuple(squares[k] for k in range(OWN)))
+    def fold(into, wide, lab):
         for k in range(OWN):
-            squares[k] = carry[k]
+            own = jnp.where(lab == first + k, wide, 0.0)
+            add = into[k]
+            for t in range(own.shape[1] // 128):
+                add = add + own[:, t * 128 : (t + 1) * 128]
+            into[k] = add
+
+    def moments(start, size):
+        at = pl.ds(pl.multiple_of(start, size), size)
+        x = ((gbuf[:, at].astype(F32) - mean_v[:, at]) * inv_v[:, at]).astype(BF16)
+        stand[:, at] = x
+        part[:, at] = jnp.dot(left_b[...], x, preferred_element_type=F32)
+
+    def square_sums(lo, hi, size):
+        def sub(s, _):
+            at = pl.ds(pl.multiple_of(s * size, size), size)
+            wide = stand[:, at].astype(F32)
+            fold(squares, jnp.sum((wide * wide).reshape(ROWS // 8, 8, size), axis=0), label_v[:, at])
+            return 0
+
+        lax.fori_loop(lo // size, hi // size, sub, 0)
 
     def unit_moments(u, _):
+        @pl.when(u + AHEAD < UNITS - 1)
+        def _():
+            geno_copy(u + AHEAD).start()
+
+        @pl.when(u + AHEAD == UNITS - 1)
+        def _():
+            last_copy.start()
+
         geno_copy(u).wait()
-        moments(u * UNIT, UNIT // SUB)
+        moments(u * UNIT, UNIT)
         return 0
 
     def units(lo, hi):
         lax.fori_loop(lo, min(hi, UNITS - 1), unit_moments, 0)
         if hi == UNITS:
             last_copy.wait()
-            moments((UNITS - 1) * UNIT, (SNPS - (UNITS - 1) * UNIT) // SUB)
+            moments((UNITS - 1) * UNIT, SNPS - (UNITS - 1) * UNIT)
 
     def half_at(g, which):
         begin, n = GROUPS[g]
@@ -167,28 +182,24 @@
         for slot in range(7):
             total = total + arrived[slot, :, slots(g)].astype(F32)
         weights[:, mine] = total.astype(BF16)
-        for hop in hops:
-            who = chip_at(hop)
+        targets = [chip_at(hop) * 2 + core for hop in hops]
+        if g in DIRECT:
+            targets = [chip_at(hop) * 2 + 1 - core for hop in hops] + targets + [chip * 2 + 1 - core]
+        for target in targets:
             pltpu.make_async_remote_copy(
                 src_ref=weights.at[:, mine], dst_ref=weights.at[:, mine],
                 send_sem=ag_send.at[g], recv_sem=ag_recv.at[g],
-                device_id=(who * 2 + core, bin_), device_id_type=MESH,
+                device_id=(target, bin_), device_id_type=MESH,
             ).start()
         trait = total[8:16, :]
         row = lax.broadcasted_iota(jnp.int32, trait.shape, 0)
         trait = jnp.where(row == PROBES - 8, trait * trait, 0.0)
-        lab = label_v[:, mine]
-        for k in range(OWN):
-            own = jnp.where(lab == first + k, trait, 0.0)
-            add = quads[k]
-            for t in range(own.shape[1] // 128):
-                add = add + own[:, t * 128 : (t + 1) * 128]
-            quads[k] = add
-
-    def seven(g):
+        fold(quads, trait, label_v[:, mine])
+
+    def gathered(g):
         begin, n = GROUPS[g]
-        half, piece = n * UNIT // 2, n * UNIT // 16
-        return weights.at[:, pl.ds(pl.multiple_of(begin * UNIT + core * half, 1024), 7 * piece)]
+        count = 15 if g in DIRECT else 7
+        return weights.at[:, pl.ds(begin * UNIT, count * n * UNIT // 16)]
 
     def half_copy(g):
         at = half_at(g, core)
@@ -199,18 +210,23 @@
         )
 
     def share(g):
-        pltpu.make_async_copy(seven(g), seven(g), ag_recv.at[g]).wait()
+        pltpu.make_async_copy(gathered(g), gathered(g), ag_recv.at[g]).wait()
         half_copy(g).start()
 
     def apply(g):
-        there = weights.at[:, half_at(g, 1 - core)]
-        pltpu.make_async_copy(there, there, half_recv.at[g]).wait()
+        if g in DIRECT:
+            pltpu.make_async_copy(gathered(g), gathered(g), ag_recv.at[g]).wait()
+        else:
+            there = weights.at[:, half_at(g, 1 - core)]
+            pltpu.make_async_copy(there, there, half_recv.at[g]).wait()
         begin, n = GROUPS[g]
         start = begin * UNIT
         stop = min(start + n * UNIT, SNPS)
 
+        size = stop - start
+
         def sub(s, acc):
-            at = pl.ds(pl.multiple_of(start + s * SUB, SUB), SUB)
+            at = pl.ds(pl.multiple_of(start + s * size, 1024), size)
             w = weights[:, at].astype(F32)
             lab = label_v[:, at]
             e = jnp.concatenate(
@@ -220,22 +236,30 @@
                 e, stand[:, at], (((1,), (1,)), ((), ())), preferred_element_type=F32
             )
 
-        hidden[...] = lax.fori_loop(0, (stop - start) // SUB, sub, hidden[...])
-
-    units(0, 5)
+        hidden[...] = lax.fori_loop(0, (stop - start) // size, sub, hidden[...])
+
+    units(0, 3)
     pl.semaphore_wait(barrier, 22)
     core_copy(0).start()
-    units(5, 7)
+    units(3, 4)
     scatter(0)
+    units(4, 6)
+    core_copy(1).start()
+    units(6, 7)
+    scatter(1)
     units(7, 9)
-    core_copy(1).start()
-    units(9, 11)
-    scatter(1)
     core_copy(2).start()
+    units(9, 10)
+    scatter(2)
+    units(10, 11)
+    core_copy(3).start()
     units(11, 12)
-    scatter(2)
+    gather(0)
     units(12, 13)
-    core_copy(3).start()
+    core_copy(4).start()
+    scatter(3)
+    gather(1)
+    scatter(4)
 
     def pick_table():
         c = lax.broadcasted_iota(jnp.int32, (256, 128), 0)
@@ -251,25 +275,21 @@
     counts = [
         jnp.sum((lab_row == first + k).astype(F32), axis=1, keepdims=True) for k in range(OWN)
     ]
-    scatter(3)
-    gather(0)
-    gather(1)
+    square_sums(0, 10240, 2560)
     gather(2)
+    square_sums(10240, SNPS, 2560)
+    share(0)
     gather(3)
-    share(0)
     share(1)
-    apply(0)
-    share(2)
-    apply(1)
-    share(3)
-    apply(2)
-    apply(3)
+    gather(4)
+    for g in range(len(GROUPS)):
+        apply(g)
 
     dense[...] = jnp.zeros_like(dense)
     for k in range(OWN):
-        f = hidden[16 * k : 16 * k + PROBES, :] / counts[k]
-        field_out[k] = f.astype(BF16)
-        dense[PROBES * k : PROBES * (k + 1), :] = f
+        dense[PROBES * k : PROBES * (k + 1), :] = (
+            hidden[16 * k : 16 * k + PROBES, :] / counts[k]
+        )
     fields[pl.ds(bin_, 1)] = dense[...].astype(BF16)[None]
     for d in (4, 3, 5, 2, 6, 1, 7):
         pltpu.make_async_remote_copy(
@@ -278,11 +298,13 @@
             device_id=(ind, lax.rem(bin_ + d, 8)), device_id_type=MESH,
         ).start()
 
+    for k in range(OWN):
+        field_out[:, k, :] = dense[PROBES * k : PROBES * (k + 1), :].astype(BF16)
+
     lane = lax.broadcasted_iota(jnp.int32, (128, 128), 1)
     extra = jnp.zeros((16, 128), F32)
     for k in range(OWN):
-        tr = squares[k][:, 0:128] + squares[k][:, 128:256]
-        extra = extra + split_dot(tr, (lane == 72 + k).astype(F32).astype(BF16))
+        extra = extra + split_dot(squares[k], (lane == 72 + k).astype(F32).astype(BF16))
         extra = extra + split_dot(quads[k], (lane == 75 + k).astype(F32).astype(BF16))
     extra = extra[0:8] + extra[8:16]
 
@@ -298,7 +320,7 @@
     gram = jnp.where(r - 10 * rk == c - 10 * ck, gram, 0.0)
     by_bin = jnp.concatenate([jnp.where(rk == k, gram, 0.0) for k in range(OWN)], axis=1)
     pairs = split_dot(by_bin, pick[...])
-    message = jnp.sum(pairs.reshape(8, 8, 128), axis=0) + extra
+    message = jnp.sum(jnp.sum(pairs.reshape(8, 8, 128), axis=0) + extra, axis=0, keepdims=True)
     messages[pl.ds(ind, 1)] = message[None]
     for d in (8, 7, 9, 6, 10, 5, 11, 4, 12, 3, 13, 2, 14, 1, 15):
         pltpu.make_async_remote_copy(
@@ -310,8 +332,9 @@
     for g in range(len(GROUPS)):
         core_copy(g).wait_send()
         pltpu.make_async_copy(all_slots(g), all_slots(g), rs_send.at[g]).wait()
-        pltpu.make_async_copy(seven(g), seven(g), ag_send.at[g]).wait()
-        half_copy(g).wait_send()
+        pltpu.make_async_copy(gathered(g), gathered(g), ag_send.at[g]).wait()
+        if g not in DIRECT:
+            half_copy(g).wait_send()
     pltpu.make_async_copy(seven_fields, seven_fields, f_send.at[0]).wait()
 
     fifteen = messages.at[0:15]
@@ -319,7 +342,6 @@
     total = messages[0]
     for i in range(1, 16):
         total = total + messages[i]
-    total = jnp.sum(total, axis=0, keepdims=True)
     for k in range(OWN):
         pair_out[k : k + 1, :] = total[:, BINS * k : BINS * (k + 1)] / (PROBES * INDIVIDUALS)
         trace_out[:, k : k + 1] = total[:, 72 + k : 73 + k] / (counts[k] * INDIVIDUALS)
@@ -327,21 +349,27 @@
     pltpu.make_async_copy(fifteen, fifteen, m_send.at[0]).wait()
 
 
+def hand_over(*refs):
+    for src, dst in zip(refs[:4], refs[4:]):
+        dst[...] = src[...]
+
+
 def shards(genotype, snp_mean, snp_scale, snp_label, probe_bits, phenotype):
     anywhere = pl.BlockSpec(memory_space=pl.ANY)
     vmem = pl.BlockSpec(memory_space=pltpu.VMEM)
     dma = pltpu.SemaphoreType.DMA
     n = len(GROUPS)
-    field, pair, trace, quad = pl.pallas_call(
+    shapes = (
+        jax.ShapeDtypeStruct((PROBES, OWN, ROWS), BF16),
+        jax.ShapeDtypeStruct((OWN, BINS), F32),
+        jax.ShapeDtypeStruct((1, OWN), F32),
+        jax.ShapeDtypeStruct((1, OWN), F32),
+    )
+    results = pl.pallas_call(
         kernel,
         name="moments_and_fields",
-        out_shape=(
-            jax.ShapeDtypeStruct((OWN, PROBES, ROWS), BF16),
-            jax.ShapeDtypeStruct((OWN, BINS), F32),
-            jax.ShapeDtypeStruct((1, OWN), F32),
-            jax.ShapeDtypeStruct((1, OWN), F32),
-        ),
-        in_specs=[anywhere] * 4 + [vmem] * 2,
+        out_shape=shapes,
+        in_specs=[anywhere] * 6,
         out_specs=(vmem,) * 4,
         scratch_shapes=[
             pltpu.VMEM((ROWS, SNPS), jnp.int32),
@@ -354,16 +382,18 @@
             pltpu.VMEM((1, SNPS), F32),
             pltpu.VMEM((1, SNPS), F32),
             pltpu.VMEM((1, PADDED), jnp.int32),
+            pltpu.VMEM((PROBES, ROWS), jnp.int32),
+            pltpu.VMEM((ROWS,), BF16),
             pltpu.VMEM((16, ROWS), F32),
             pltpu.VMEM((16, ROWS), BF16),
-            pltpu.VMEM((OWN, 8, SUB), F32),
+            pltpu.VMEM((OWN, 8, 128), F32),
             pltpu.VMEM((OWN, 8, 128), F32),
             pltpu.VMEM((16 * OWN, ROWS), F32),
             pltpu.VMEM((32, ROWS), F32),
             pltpu.VMEM((8, 32, ROWS), BF16),
-            pltpu.VMEM((16, 8, 128), F32),
+            pltpu.VMEM((16, 1, 128), F32),
             pltpu.VMEM((768, 128), BF16),
-            dma((UNITS,)), dma((3,)),
+            dma((UNITS,)), dma((5,)),
             dma((n,)), dma((n,)), dma((n,)), dma((n,)), dma((n,)), dma((n,)), dma((n,)), dma((n,)),
             dma((1,)), dma((1,)), dma((1,)), dma((1,)),
         ],
@@ -379,9 +409,12 @@
         snp_scale.reshape(1, -1),
         snp_label.reshape(1, -1),
         probe_bits,
-        phenotype.reshape(1, -1),
+        phenotype,
     )
-    return field, pair, trace.reshape(-1), quad.reshape(-1)
+    field, pair, trace, quad = pl.pallas_call(
+        hand_over, name="hand_over", out_shape=shapes, in_specs=[vmem] * 4, out_specs=(vmem,) * 4
+    )(*results)
+    return field.transpose(1, 0, 2), pair, trace.reshape(-1), quad.reshape(-1)
 
 
 def solution(mesh):

time: 77.5 us -> 42.8 us (0.55)
  Pallas kernels: 70.5 us -> 42 us
  local copies, waits for them, and re-layouts: 6.08 us -> 0 us
    pallas_call x1 -> x2, Pallas kernels: 70.5 us -> 42 us  [the longest x1 40.6 us: shards(): pl.pallas_call(kernel, name='moments_and_fields', out_shape=shapes, in_sp...]
    unnamed x4 -> x0, local copies, waits for them, and re-layouts: 4.86 us -> none
    reshape x1 -> x0, local copies, waits for them, and re-layouts: 1.22 us -> none  [shards(): phenotype.reshape(1, -1)]
where the time goes in v2:
time: 42.8 us; the launch traced here: 42.6 us
  Pallas kernels  42 us (98%)
  between operations  0.64 us (1%)
    pallas_call x1, Pallas kernels, shards(): pl.pallas_call(kernel, name='moments_and_fields', out_shape=shapes, in_sp...  40.6 us
    pallas_call x1, Pallas kernels, shards(): pl.pallas_call(hand_over, name='hand_over', out_shape=shapes, in_specs=[v...  1.36 us

profile of v2, /device:TPU:1, one launch (start us, length us, event | category | flops | bytes accessed | tf_op | source)
XLA Modules:
  0.0 42.6 jit_solution(2251183736148538252)
XLA Ops:
  0.6 40.6 %moments_and_fields.1 = (bf16[10,3,256]{2,1,0:T(4,128)(2,1)}, f32[3,24]{1,0:T(4,128)}, f32[1,3]{1,0:T(1,128)}, f32[1,3]{1,0:T(1,128)}) custom-call(s32[256,25600]{1,0:T(8,128)} %geno.1, f32[1,25600]{1,0:T(1,128)} %bitcast.6, f32[1,25600]{1,0:T(1,128)} %bitcast.7, s32[1,25600]{1,0:T(1,128)} %bitcast.8, s32[10,256]{1,0:T(8,128)} %probes.1, bf16[256]{0:T(256)(128)(2,1)} %pheno.1), custom_call_target="tpu_custom_call" | custom-call | flops 838860800 | bytes 26214400 | tf_op jit(solution)/shard_map/moments_and_fields/pallas_call | solution.py:368
  41.2 1.4 %hand_over.1 = (bf16[10,3,256]{2,1,0:T(4,128)(2,1)}, f32[3,24]{1,0:T(4,128)}, f32[1,3]{1,0:T(1,128)}, f32[1,3]{1,0:T(1,128)}) custom-call(bf16[10,3,256]{2,1,0:T(4,128)(2,1)} %get-tuple-element.12.refs_0_, f32[3,24]{1,0:T(4,128)} %get-tuple-element.13.refs_1_, f32[1,3]{1,0:T(1,128)} %get-tuple-element.14.refs_2_, f32[1,3]{1,0:T(1,128)} %get-tuple-element.15.refs_3_), custom_call_target="tpu_custom_call" | custom-call | tf_op jit(solution)/shard_map/hand_over/pallas_call | solution.py:414

commit v3 on v2

--- a/solution.py
+++ b/solution.py
@@ -35,7 +35,7 @@
     geno, mean, scale, label, probes, pheno,
     field_out, pair_out, trace_out, quad_out,
     gbuf, stand, part, other, sums, arrived, weights,
-    mean_v, inv_v, label_v, probes_v, pheno_v, left_f, left_b, squares, quads, hidden, dense, fields, messages, pick,
+    mean_v, inv_v, label_v, probes_v, pheno_v, left_f, left_b, squares, quads, share_v, hidden, dense, fields, messages, pick,
     g_sem, s_sem, core_send, core_recv, rs_send, rs_recv, ag_send, ag_recv, half_send, half_recv,
     f_send, f_recv, m_send, m_recv,
 ):
@@ -182,9 +182,13 @@
         for slot in range(7):
             total = total + arrived[slot, :, slots(g)].astype(F32)
         weights[:, mine] = total.astype(BF16)
-        targets = [chip_at(hop) * 2 + core for hop in hops]
+        targets = []
+        for hop in hops:
+            if g in DIRECT:
+                targets.append(chip_at(hop) * 2 + 1 - core)
+            targets.append(chip_at(hop) * 2 + core)
         if g in DIRECT:
-            targets = [chip_at(hop) * 2 + 1 - core for hop in hops] + targets + [chip * 2 + 1 - core]
+            targets.append(chip * 2 + 1 - core)
         for target in targets:
             pltpu.make_async_remote_copy(
                 src_ref=weights.at[:, mine], dst_ref=weights.at[:, mine],
@@ -272,30 +276,36 @@
 
     pick_table()
     lab_row = label_v[:, 0:SNPS]
-    counts = [
-        jnp.sum((lab_row == first + k).astype(F32), axis=1, keepdims=True) for k in range(OWN)
-    ]
+    for k in range(OWN):
+        count = jnp.sum((lab_row == first + k).astype(F32), axis=1, keepdims=True)
+        share_v[k : k + 1, :] = jnp.broadcast_to(1.0 / count, (1, 128))
     square_sums(0, 10240, 2560)
     gather(2)
     square_sums(10240, SNPS, 2560)
     share(0)
     gather(3)
+    apply(0)
     share(1)
     gather(4)
-    for g in range(len(GROUPS)):
-        apply(g)
-
+    apply(1)
+    apply(2)
+    apply(3)
+    apply(4)
+
+    shares = [share_v[k : k + 1, 0:1] for k in range(OWN)]
     dense[...] = jnp.zeros_like(dense)
     for k in range(OWN):
         dense[PROBES * k : PROBES * (k + 1), :] = (
-            hidden[16 * k : 16 * k + PROBES, :] / counts[k]
+            hidden[16 * k : 16 * k + PROBES, :] * shares[k]
         )
     fields[pl.ds(bin_, 1)] = dense[...].astype(BF16)[None]
-    for d in (4, 3, 5, 2, 6, 1, 7):
+    bz, by = bin_ // 4, lax.rem(bin_, 4)
+    for dz, dy in ((1, 2), (1, 1), (1, 3), (0, 2), (1, 0), (0, 1), (0, 3)):
+        target = lax.rem(bz + dz, 2) * 4 + lax.rem(by + dy, 4)
         pltpu.make_async_remote_copy(
             src_ref=fields.at[bin_], dst_ref=fields.at[bin_],
             send_sem=f_send.at[0], recv_sem=f_recv.at[0],
-            device_id=(ind, lax.rem(bin_ + d, 8)), device_id_type=MESH,
+            device_id=(ind, target), device_id_type=MESH,
         ).start()
 
     for k in range(OWN):
@@ -307,6 +317,11 @@
         extra = extra + split_dot(squares[k], (lane == 72 + k).astype(F32).astype(BF16))
         extra = extra + split_dot(quads[k], (lane == 75 + k).astype(F32).astype(BF16))
     extra = extra[0:8] + extra[8:16]
+
+    lane = lax.broadcasted_iota(jnp.int32, (1, 128), 1)
+    factors = jnp.full((1, 128), 1.0 / (PROBES * INDIVIDUALS), F32)
+    for k in range(OWN):
+        factors = jnp.where((lane == 72 + k) | (lane == 75 + k), shares[k] / INDIVIDUALS, factors)
 
     seven_fields = fields.at[0:7]
     pltpu.make_async_copy(seven_fields, seven_fields, f_recv.at[0]).wait()
@@ -322,11 +337,12 @@
     pairs = split_dot(by_bin, pick[...])
     message = jnp.sum(jnp.sum(pairs.reshape(8, 8, 128), axis=0) + extra, axis=0, keepdims=True)
     messages[pl.ds(ind, 1)] = message[None]
-    for d in (8, 7, 9, 6, 10, 5, 11, 4, 12, 3, 13, 2, 14, 1, 15):
+    others = [chip_at(hop) * 2 + c for hop in hops for c in (1 - core, core)]
+    for target in others + [chip * 2 + 1 - core]:
         pltpu.make_async_remote_copy(
             src_ref=messages.at[ind], dst_ref=messages.at[ind],
             send_sem=m_send.at[0], recv_sem=m_recv.at[0],
-            device_id=(lax.rem(ind + d, 16), bin_), device_id_type=MESH,
+            device_id=(target, bin_), device_id_type=MESH,
         ).start()
 
     for g in range(len(GROUPS)):
@@ -342,10 +358,11 @@
     total = messages[0]
     for i in range(1, 16):
         total = total + messages[i]
-    for k in range(OWN):
-        pair_out[k : k + 1, :] = total[:, BINS * k : BINS * (k + 1)] / (PROBES * INDIVIDUALS)
-        trace_out[:, k : k + 1] = total[:, 72 + k : 73 + k] / (counts[k] * INDIVIDUALS)
-        quad_out[:, k : k + 1] = total[:, 75 + k : 76 + k] / (counts[k] * INDIVIDUALS)
+    total = total * factors
+    for k in range(OWN):
+        pair_out[k : k + 1, :] = total[:, BINS * k : BINS * (k + 1)]
+    trace_out[...] = total[:, 72 : 72 + OWN]
+    quad_out[...] = total[:, 75 : 75 + OWN]
     pltpu.make_async_copy(fifteen, fifteen, m_send.at[0]).wait()
 
 
@@ -388,6 +405,7 @@
             pltpu.VMEM((16, ROWS), BF16),
             pltpu.VMEM((OWN, 8, 128), F32),
             pltpu.VMEM((OWN, 8, 128), F32),
+            pltpu.VMEM((8, 128), F32),
             pltpu.VMEM((16 * OWN, ROWS), F32),
             pltpu.VMEM((32, ROWS), F32),
             pltpu.VMEM((8, 32, ROWS), BF16),

time: 42.8 us -> 41.9 us (0.979)
  Pallas kernels: 42 us -> 41.1 us
    pallas_call x1, Pallas kernels: 40.6 us -> 39.8 us  [shards(): pl.pallas_call(kernel, name='moments_and_fields', out_shape=shapes, in_sp...]
where the time goes in v3:
time: 41.9 us; the launch traced here: 41.8 us
  Pallas kernels  41.1 us (98%)
  between operations  0.64 us (2%)
    pallas_call x1, Pallas kernels, shards(): pl.pallas_call(kernel, name='moments_and_fields', out_shape=shapes, in_sp...  39.8 us
    pallas_call x1, Pallas kernels, shards(): pl.pallas_call(hand_over, name='hand_over', out_shape=shapes, in_specs=[v...  1.36 us

profile of v3, /device:TPU:1, one launch (start us, length us, event | category | flops | bytes accessed | tf_op | source)
XLA Modules:
  0.0 41.8 jit_solution(11269304837155021)
XLA Ops:
  0.6 39.8 %moments_and_fields.1 = (bf16[10,3,256]{2,1,0:T(4,128)(2,1)}, f32[3,24]{1,0:T(4,128)}, f32[1,3]{1,0:T(1,128)}, f32[1,3]{1,0:T(1,128)}) custom-call(s32[256,25600]{1,0:T(8,128)} %geno.1, f32[1,25600]{1,0:T(1,128)} %bitcast.6, f32[1,25600]{1,0:T(1,128)} %bitcast.7, s32[1,25600]{1,0:T(1,128)} %bitcast.8, s32[10,256]{1,0:T(8,128)} %probes.1, bf16[256]{0:T(256)(128)(2,1)} %pheno.1), custom_call_target="tpu_custom_call" | custom-call | flops 838860800 | bytes 26214400 | tf_op jit(solution)/shard_map/moments_and_fields/pallas_call | solution.py:385
  40.4 1.4 %hand_over.1 = (bf16[10,3,256]{2,1,0:T(4,128)(2,1)}, f32[3,24]{1,0:T(4,128)}, f32[1,3]{1,0:T(1,128)}, f32[1,3]{1,0:T(1,128)}) custom-call(bf16[10,3,256]{2,1,0:T(4,128)(2,1)} %get-tuple-element.12.refs_0_, f32[3,24]{1,0:T(4,128)} %get-tuple-element.13.refs_1_, f32[1,3]{1,0:T(1,128)} %get-tuple-element.14.refs_2_, f32[1,3]{1,0:T(1,128)} %get-tuple-element.15.refs_3_), custom_call_target="tpu_custom_call" | custom-call | tf_op jit(solution)/shard_map/hand_over/pallas_call | solution.py:432

commit v4 on v3

--- a/solution.py
+++ b/solution.py
@@ -16,7 +16,7 @@
 UNIT = 2048
 PADDED = 26624
 UNITS = 13
-AHEAD = 3
+AHEAD = 4
 GROUPS = ((0, 3), (3, 3), (6, 3), (9, 2), (11, 2))
 DIRECT = (2, 3, 4)
 F32 = jnp.float32
@@ -33,11 +33,11 @@
 
 def kernel(
     geno, mean, scale, label, probes, pheno,
-    field_out, pair_out, trace_out, quad_out,
+    field_out, row_out,
     gbuf, stand, part, other, sums, arrived, weights,
-    mean_v, inv_v, label_v, probes_v, pheno_v, left_f, left_b, squares, quads, share_v, hidden, dense, fields, messages, pick,
+    mean_v, inv_v, label_v, probes_v, pheno_v, left_f, left_b, squares, quads, share_v, hidden, dense, fields, messages, pick, field_v,
     g_sem, s_sem, core_send, core_recv, rs_send, rs_recv, ag_send, ag_recv, half_send, half_recv,
-    f_send, f_recv, m_send, m_recv,
+    f_send, f_recv, m_send, m_recv, out_sem,
 ):
     ind = lax.axis_index("ind")
     bin_ = lax.axis_index("bin")
@@ -53,9 +53,6 @@
         pltpu.make_async_copy(probes, probes_v, s_sem.at[3]),
         pltpu.make_async_copy(pheno, pheno_v, s_sem.at[4]),
     ]
-    for copy in small:
-        copy.start()
-
     def geno_copy(u):
         at = pl.ds(pl.multiple_of(u * UNIT, UNIT), UNIT)
         return pltpu.make_async_copy(geno.at[:, at], gbuf.at[:, at], g_sem.at[u])
@@ -63,7 +60,9 @@
     last_at = pl.ds((UNITS - 1) * UNIT, SNPS - (UNITS - 1) * UNIT)
     last_copy = pltpu.make_async_copy(geno.at[:, last_at], gbuf.at[:, last_at], g_sem.at[UNITS - 1])
     for u in range(AHEAD):
-        geno_copy(u).start()
+        geno_copy(u).start(priority=1)
+    for copy in small:
+        copy.start()
 
     barrier = pltpu.get_barrier_semaphore()
     for d in range(1, 16):
@@ -114,11 +113,11 @@
     def unit_moments(u, _):
         @pl.when(u + AHEAD < UNITS - 1)
         def _():
-            geno_copy(u + AHEAD).start()
+            geno_copy(u + AHEAD).start(priority=1)
 
         @pl.when(u + AHEAD == UNITS - 1)
         def _():
-            last_copy.start()
+            last_copy.start(priority=1)
 
         geno_copy(u).wait()
         moments(u * UNIT, UNIT)
@@ -309,7 +308,9 @@
         ).start()
 
     for k in range(OWN):
-        field_out[:, k, :] = dense[PROBES * k : PROBES * (k + 1), :].astype(BF16)
+        field_v[:, k, :] = dense[PROBES * k : PROBES * (k + 1), :].astype(BF16)
+    field_copy = pltpu.make_async_copy(field_v, field_out, out_sem.at[0])
+    field_copy.start()
 
     lane = lax.broadcasted_iota(jnp.int32, (128, 128), 1)
     extra = jnp.zeros((16, 128), F32)
@@ -358,17 +359,17 @@
     total = messages[0]
     for i in range(1, 16):
         total = total + messages[i]
-    total = total * factors
-    for k in range(OWN):
-        pair_out[k : k + 1, :] = total[:, BINS * k : BINS * (k + 1)]
-    trace_out[...] = total[:, 72 : 72 + OWN]
-    quad_out[...] = total[:, 75 : 75 + OWN]
+    row_out[...] = total * factors
+    field_copy.wait()
     pltpu.make_async_copy(fifteen, fifteen, m_send.at[0]).wait()
 
 
-def hand_over(*refs):
-    for src, dst in zip(refs[:4], refs[4:]):
-        dst[...] = src[...]
+def hand_over(field, row, field_out, pair_out, trace_out, quad_out):
+    field_out[...] = field[...]
+    for k in range(OWN):
+        pair_out[k : k + 1, :] = row[:, BINS * k : BINS * (k + 1)]
+    trace_out[...] = row[:, 72 : 72 + OWN]
+    quad_out[...] = row[:, 75 : 75 + OWN]
 
 
 def shards(genotype, snp_mean, snp_scale, snp_label, probe_bits, phenotype):
@@ -385,9 +386,9 @@
     results = pl.pallas_call(
         kernel,
         name="moments_and_fields",
-        out_shape=shapes,
+        out_shape=(shapes[0], jax.ShapeDtypeStruct((1, 128), F32)),
         in_specs=[anywhere] * 6,
-        out_specs=(vmem,) * 4,
+        out_specs=(anywhere, vmem),
         scratch_shapes=[
             pltpu.VMEM((ROWS, SNPS), jnp.int32),
             pltpu.VMEM((ROWS, SNPS), BF16),
@@ -411,9 +412,10 @@
             pltpu.VMEM((8, 32, ROWS), BF16),
             pltpu.VMEM((16, 1, 128), F32),
             pltpu.VMEM((768, 128), BF16),
+            pltpu.VMEM((PROBES, OWN, ROWS), BF16),
             dma((UNITS,)), dma((5,)),
             dma((n,)), dma((n,)), dma((n,)), dma((n,)), dma((n,)), dma((n,)), dma((n,)), dma((n,)),
-            dma((1,)), dma((1,)), dma((1,)), dma((1,)),
+            dma((1,)), dma((1,)), dma((1,)), dma((1,)), dma((1,)),
         ],
         compiler_params=pltpu.CompilerParams(
             collective_id=0, has_side_effects=True, vmem_limit_bytes=58 * 2**20
@@ -430,7 +432,7 @@
         phenotype,
     )
     field, pair, trace, quad = pl.pallas_call(
-        hand_over, name="hand_over", out_shape=shapes, in_specs=[vmem] * 4, out_specs=(vmem,) * 4
+        hand_over, name="hand_over", out_shape=shapes, in_specs=[vmem] * 2, out_specs=(vmem,) * 4
     )(*results)
     return field.transpose(1, 0, 2), pair, trace.reshape(-1), quad.reshape(-1)
 

time: 41.9 us -> 41.8 us (level)
  no operation moved by 1% of the time
where the time goes in v4:
time: 41.8 us; the launch traced here: 41.6 us
  Pallas kernels  41 us (98%)
  between operations  0.64 us (2%)
    pallas_call x1, Pallas kernels, shards(): pl.pallas_call(kernel, name='moments_and_fields', out_shape=(shapes[0], j...  39.6 us
    pallas_call x1, Pallas kernels, shards(): pl.pallas_call(hand_over, name='hand_over', out_shape=shapes, in_specs=[v...  1.38 us

profile of v4, /device:TPU:1, one launch (start us, length us, event | category | flops | bytes accessed | tf_op | source)
XLA Modules:
  0.0 41.6 jit_solution(11355072851136651223)
XLA Ops:
  0.6 39.6 %moments_and_fields.1 = (bf16[10,3,256]{2,1,0:T(4,128)(2,1)}, f32[1,128]{1,0:T(1,128)}) custom-call(s32[256,25600]{1,0:T(8,128)} %geno.1, f32[1,25600]{1,0:T(1,128)} %bitcast.6, f32[1,25600]{1,0:T(1,128)} %bitcast.7, s32[1,25600]{1,0:T(1,128)} %bitcast.8, s32[10,256]{1,0:T(8,128)} %probes.1, bf16[256]{0:T(256)(128)(2,1)} %pheno.1), custom_call_target="tpu_custom_call" | custom-call | flops 838860800 | bytes 26214400 | tf_op jit(solution)/shard_map/moments_and_fields/pallas_call | solution.py:386
  40.3 1.4 %hand_over.1 = (bf16[10,3,256]{2,1,0:T(4,128)(2,1)}, f32[3,24]{1,0:T(4,128)}, f32[1,3]{1,0:T(1,128)}, f32[1,3]{1,0:T(1,128)}) custom-call(bf16[10,3,256]{2,1,0:T(4,128)(2,1)} %get-tuple-element.10.field, f32[1,128]{1,0:T(1,128)} %get-tuple-element.11.row), custom_call_target="tpu_custom_call" | custom-call | tf_op jit(solution)/shard_map/hand_over/pallas_call | solution.py:434
